TPU v7x, 128 devices: a whole 4x4x4 slice. The times are simulated.
128 devices in a mesh: row: 8 (over z, core), col: 16 (over x, y).
Axes of the slice: x: 4, y: 4, z: 4, core: 2. Of those that a mesh axis runs over, the one named last changes fastest.
Arguments:
- tensor: bfloat16 [128, 1024, 4096], P('row', 'col'), may hold values from -6 to 6
- pair_mu: int32 [1024], P('col'), may hold values from 0 to 15, as said below
- pair_nu: int32 [1024], P('col'), may hold values from 0 to 127, as said below
- occ_density: bfloat16 [8192, 384], replicated, may hold values from -0.09375 to 0.09375
- virt_density: bfloat16 [1024, 128], P('row'), may hold values from -0.5 to 0.5
Outputs:
- transformed: bfloat16 [8, 16, 1024, 384], P(None, 'col', 'row')
Inputs may be any that keep to these rules, and one draw needn't show every extreme that they name: `pair_mu`: within the 64 pairs of one index of col (aligned runs of the list), at most 8 pairs name one mu block, and in every such run some mu block is named by exactly 8. `pair_nu`: no two pairs name the same mu block and the same nu block.
All inputs are finite; a program needn't handle non-finite values.
Results may differ from a plain program's by a relative error of at most 0.005.
Values may be sent and summed in bfloat16 or wider, within the bound.
A program may use at most 192 MiB of HBM per device.

v0:
```python
import jax
import jax.numpy as jnp
from jax import lax
from jax.sharding import PartitionSpec as P

BS = 64
CAPM = 8
NBNU = 128
NNU = 384


def bucket_slots(pair_mu, pair_nu, block_count, capacity):
    pair_count = pair_mu.shape[0]
    block_ids = jnp.arange(block_count, dtype=jnp.int32)
    member = (pair_mu[:, None] == block_ids[None, :]).astype(jnp.int32)
    ranking = jnp.sum(member * (jnp.cumsum(member, axis=0) - 1), axis=1)
    places = jnp.arange(capacity, dtype=jnp.int32)
    matches = (pair_mu[None, None, :] == block_ids[:, None, None]) & (
        ranking[None, None, :] == places[None, :, None]
    )
    matches = matches.astype(jnp.int32)
    position = jnp.arange(pair_count, dtype=jnp.int32)
    source = jnp.sum(matches * position[None, None, :], axis=2)
    filled = jnp.sum(matches, axis=2)
    target = jnp.sum(matches * pair_nu[None, None, :], axis=2)
    return (source, filled, target)


def local(tensor, pair_mu, pair_nu, occ_density, virt_density):
    row_count = lax.axis_size("row")
    aux_rows = tensor.shape[0]
    flat_size = tensor.shape[2]
    source, filled, target = bucket_slots(pair_mu, pair_nu, 2 * row_count, CAPM)
    picked = jnp.take(tensor, source.reshape(-1), axis=1)
    picked = picked * filled.reshape(1, -1, 1).astype(picked.dtype)
    occ_table = occ_density.reshape(NBNU, BS, NNU)
    own_row = lax.axis_index("row")
    own_ids = lax.dynamic_slice_in_dim(target.reshape(row_count, 2 * CAPM), own_row, 1, 0)
    packed = picked.reshape(1, aux_rows, row_count, 2 * CAPM, flat_size)
    arrived = lax.all_to_all(packed, "row", split_axis=2, concat_axis=0, tiled=True)
    blocks_in = arrived.reshape(row_count, aux_rows, 2, CAPM, BS, BS)
    selected = jnp.take(occ_table, own_ids.reshape(-1), axis=0).reshape(2, CAPM, BS, NNU)
    partial_sum = jnp.einsum(
        "raqkij,qkjo->raqio", blocks_in, selected, preferred_element_type=jnp.float32
    )
    summed = lax.psum_scatter(partial_sum, "col", scatter_dimension=1, tiled=True)
    summed_bf = summed.reshape(row_count, summed.shape[1], 2 * BS, NNU).astype(jnp.bfloat16)
    transformed = jnp.einsum(
        "ki,rain->rakn", virt_density, summed_bf, preferred_element_type=jnp.float32
    )
    return transformed.astype(jnp.bfloat16)


def solution(mesh):
    placed = (P("row", "col", None), P("col"), P("col"), P(), P("row", None))
    return jax.shard_map(
        local, mesh=mesh, in_specs=placed, out_specs=P(None, "col", "row", None), check_vma=False
    )
```

profile of v0, /device:TPU:1, one launch (start us, length us, event | category | flops | bytes accessed | tf_op | source)
XLA Modules:
  0.0 853.5 jit_solution(12176216276855455525)
XLA Ops:
  0.0 0.0 copy-start
  0.0 0.7 fusion.15
  0.7 0.7 iota_compare_fusion.1
  1.4 0.1 reduce_window_sum.11
  1.5 0.8 select_reduce_fusion
  2.3 1.6 fusion.11
  3.9 0.1 reshape.181
  4.0 0.1 reshape.180
  4.1 0.1 convert_element_type.38
  4.2 34.3 %gather_fusion.1 = bf16[128,16,4096]{2,0,1:T(8,128)(2,1)} fusion(bf16[16,64,4096]{2,1,0:T(8,128)(2,1)} %param.5, s32[1024]{0:T(1024)S(1)} %pad_clamp_fusion), kind=kCustom, calls=%fused_computation.1 | custom fusion | bytes 33554944 | tf_op jit(solution)/shard_map/jit(_take)/gather | solution.py:34
  38.4 14.2 %fusion.2 = bf16[1,16,8,16,4096]{4,3,1,0,2:T(8,128)(2,1)} fusion(bf16[1,16,8,16,4096]{4,3,2,1,0:T(8,128)(2,1)} %bitcast.46, pred[8,16]{1,0:T(8,128)(4,1)S(1)} %compare_and_fusion, bf16[8,16]{1,0:T(8,128)(2,1)S(1)} %convert_element_type.38), kind=kLoop, calls=%fused_computation.5 | loop fusion | flops 16777216 | bytes 33554816 | tf_op jit(solution)/shard_map/mul | solution.py:35
  52.6 0.0 copy-start.1
  52.6 7.1 all-to-all-start
  59.8 0.1 reshape.176
  59.9 0.1 reshape.177
  60.0 3.5 gather_fusion
  63.5 0.0 copy-done.1
  63.5 0.6 dynamic-slice
  64.1 179.3 %all-to-all-done = bf16[1,16,8,16,4096]{4,3,1,0,2:T(8,128)(2,1)} async-done(((bf16[1,16,8,16,4096]{4,3,1,0,2:T(8,128)(2,1)}), bf16[1,16,8,16,4096]{4,3,1,0,2:T(8,128)(2,1)}, u32[]{:S(2)}, u32[]{:S(2)}) %all-to-all-start) | async-done | bytes 16777248 | tf_op jit(solution)/shard_map/all_to_all | solution.py:40
  243.4 46.0 %reshape.182 = bf16[8,16,2,8,64,64]{5,4,3,2,1,0:T(8,128)(2,1)} reshape(bf16[8,1,16,1,16,4096]{5,4,2,0,3,1:T(8,128)(2,1)} %bitcast.10) | data formatting | bytes 33554432 | tf_op jit(solution)/shard_map/reshape | solution.py:41
  289.4 21.2 %fusion.3 = f32[8,16,2,64,384]{4,3,1,0,2:T(8,128)} fusion(bf16[8,16,2,8,64,64]{5,4,3,2,1,0:T(8,128)(2,1)} %reshape.182, bf16[2,8,64,384]{3,2,1,0:T(8,128)(2,1)S(1)} %bitcast.48, pred[2,8]{1,0:T(4,128)(4,1)S(1)} %compare_and_fusion.1), kind=kOutput, calls=%fused_computation.6 | convolution fusion | flops 6442844160 | bytes 42729488 | tf_op jit(solution)/shard_map/raqkij,qkjo->raqio/dot_general | solution.py:43
  310.5 539.5 %all-reduce.2 = bf16[8,16,2,64,384]{4,3,1,0,2:T(8,128)(2,1)} all-reduce(f32[8,16,2,64,384]{4,3,1,0,2:T(8,128)} %fusion.3), channel_id=2, replica_groups=mesh['row'=8,'col'=16] {'col'}, use_global_device_ids=true, to_apply=%region_5.6.clone | all-reduce | flops 6291456 | bytes 37748736
  850.0 1.9 constant_dynamic-slice_fusion
  851.9 0.1 copy.35
  852.0 0.0 copy-done
  852.0 0.4 fusion.6
  852.4 1.2 copy.21
  (9 shorter events, 0.1 us)
Async XLA Ops:
  0.0 852.0 %copy-start = (bf16[128,128]{1,0:T(8,128)(2,1)S(1)}, bf16[128,128]{1,0:T(8,128)(2,1)}, u32[]{:S(2)}) copy-start(bf16[128,128]{1,0:T(8,128)(2,1)} %param.9) | copy-start | bytes 98308
  52.6 10.9 %copy-start.1 = (u32[128]{0:T(128)S(1)}, u32[128]{0:T(128)}, u32[]{:S(2)}) copy-start(u32[128]{0:T(128)} %constant.50) | copy-start | bytes 1540
  52.6 190.7 %all-to-all-start = ((bf16[1,16,8,16,4096]{4,3,1,0,2:T(8,128)(2,1)}), bf16[1,16,8,16,4096]{4,3,1,0,2:T(8,128)(2,1)}, u32[]{:S(2)}, u32[]{:S(2)}) async-start(bf16[1,16,8,16,4096]{4,3,1,0,2:T(8,128)(2,1)} %fusion.2), calls=%async_computation | async-start | bytes 33554432 | tf_op jit(solution)/shard_map/all_to_all | solution.py:40
where the time goes:
time: 857 us; the launch traced here: 854 us
  blocking collectives  539 us (63%)
  waiting for transfers between devices  179 us (21%)
  local copies, waits for them, and re-layouts  87.9 us (10%)
  matrix products  21.6 us (3%)
  other arithmetic  18.1 us (2%)
    unnamed x1, blocking collectives  539 us
    all_to_all x1, waiting for transfers between devices, local(): lax.all_to_all(packed, 'row', split_axis=2, concat_axis=0, tiled=True)  179 us
    reshape x1, local copies, waits for them, and re-layouts, local(): blocks_in = arrived.reshape(row_count, aux_rows, 2, CAPM, BS, BS)  46 us
    gather x1, local copies, waits for them, and re-layouts, local(): picked = jnp.take(tensor, source.reshape(-1), axis=1)  34.3 us
    dot_general x1, matrix products, local(): jnp.einsum('raqkij,qkjo->raqio', blocks_in, selected, preferred_element_t...  21.2 us
  transfers between devices with their start and end apart: 1, of which 1 were waited for; matrix products, arithmetic and copies ran while one was open for 1% of the time, Pallas kernels for 0%

commit v1 on v0

v1 whole, which is shorter than its diff:
```python
import jax
import jax.numpy as jnp
from jax import lax
from jax.experimental import pallas as pl
from jax.experimental.pallas import tpu as pltpu
from jax.sharding import PartitionSpec as P

MESH = pl.DeviceIdType.MESH
BS = 64
NNU = 384
NBNU = 128
NMB = 16
CAPM = 8
PAIRS = 64
HALF = 2048
ORDER = (2, 1, 3, 0)
F32 = jnp.float32
BF16 = jnp.bfloat16


def slot_table(mu_row, nu_row):
    sub = lax.broadcasted_iota(jnp.int32, (PAIRS, PAIRS), 0)
    lane = lax.broadcasted_iota(jnp.int32, (PAIRS, PAIRS), 1)
    mu_b = jnp.broadcast_to(mu_row, (PAIRS, PAIRS))
    nu_b = jnp.broadcast_to(nu_row, (PAIRS, PAIRS))
    mu_col = jnp.sum(jnp.where(sub == lane, mu_b, 0), axis=1, keepdims=True)
    nu_col = jnp.sum(jnp.where(sub == lane, nu_b, 0), axis=1, keepdims=True)
    rank = jnp.sum(jnp.where((mu_b == mu_col) & (lane < sub), 1, 0), axis=1, keepdims=True)
    slot = lax.broadcasted_iota(jnp.int32, (PAIRS, NMB * CAPM), 1)
    pair = lax.broadcasted_iota(jnp.int32, (PAIRS, NMB * CAPM), 0)
    hit = (mu_col * CAPM + rank) == slot
    source = jnp.sum(jnp.where(hit, pair, 0), axis=0, keepdims=True)
    target = jnp.sum(jnp.where(hit, nu_col - NBNU, 0), axis=0, keepdims=True) + NBNU
    row = lax.broadcasted_iota(jnp.int32, (8, NMB * CAPM), 0)
    return jnp.where(row == 0, source, target)


def kernel(t_ref, mu_ref, nu_ref, occ_ref, virt_ref, o_ref,
           arrived, occ, zbuf, xt, sums, sbuf, rbuf, hbuf, gbuf, tab_v, tab_r, tab_s,
           occ_sem, own_sem, s1, r1, st, rt, tab_sem, s2, r2, s3, r3, loc_sem):
    row, col = lax.axis_index("row"), lax.axis_index("col")
    x, y, z, core = col // 4, col % 4, row // 2, row % 2

    def at_x(d):
        return (row, lax.rem(x + d, 4) * 4 + y)

    def at_y(d):
        return (row, x * 4 + lax.rem(y + d, 4))

    def ring(h, d):
        return at_x(d) if h == 0 else at_y(d)

    occ_copy = pltpu.make_async_copy(occ_ref, occ.at[pl.ds(0, NBNU)], occ_sem)
    occ_copy.start()

    def piece(h, d):
        if h == 0:
            return t_ref.at[lax.rem(x + d, 4), :, :, pl.ds(0, HALF)]
        return t_ref.at[:, lax.rem(y + d, 4), :, pl.ds(HALF, HALF)]

    own = []
    for h in range(2):
        copy = pltpu.make_async_copy(piece(h, 0), arrived.at[h], own_sem.at[h])
        copy.start()
        own.append(copy)

    barrier = pltpu.get_barrier_semaphore()
    for d in range(1, 4):
        pl.semaphore_signal(barrier, inc=1, device_id=at_x(d), device_id_type=MESH)
        pl.semaphore_signal(barrier, inc=1, device_id=at_y(d), device_id_type=MESH)
    for d in range(1, 8):
        pl.semaphore_signal(barrier, inc=1, device_id=(lax.rem(row + d, 8), col), device_id_type=MESH)
    pl.semaphore_wait(barrier, 13)

    sends = []
    for d in (1, 3, 2):
        for h in range(2):
            u = d * 2 + h
            copy = pltpu.make_async_remote_copy(
                src_ref=piece(h, d), dst_ref=arrived.at[u], send_sem=s1.at[u], recv_sem=r1.at[u],
                device_id=ring(h, d), device_id_type=MESH)
            copy.start()
            sends.append(copy)

    tab_v[...] = slot_table(mu_ref[...], nu_ref[...])
    tab_r[0] = tab_v[...]
    tab_r[1] = tab_v[...]
    for d in (1, 3, 2):
        for h in range(2):
            u = d * 2 + h
            copy = pltpu.make_async_remote_copy(
                src_ref=tab_v, dst_ref=tab_r.at[u], send_sem=st.at[u], recv_sem=rt.at[u],
                device_id=ring(h, d), device_id_type=MESH)
            copy.start()
            sends.append(copy)
    occ[NBNU] = jnp.zeros((BS, NNU), BF16)
    for copy in sends[6:]:
        copy.wait_recv()
    tab_copy = pltpu.make_async_copy(tab_r, tab_s, tab_sem)
    tab_copy.start()
    c = lax.broadcasted_iota(jnp.int32, (128, 128), 1)
    r = lax.broadcasted_iota(jnp.int32, (128, 128), 0)
    from_col = (c // 64) * 64 + ((c // 32) % 2) * 32 + (c % 16) * 2 + (c // 16) % 2
    perm = jnp.where(r == from_col, 1.0, 0.0).astype(BF16)
    virt = jnp.dot(virt_ref[...], perm, preferred_element_type=F32).astype(BF16)
    tab_copy.wait()
    occ_copy.wait()

    def relayout(u, b):
        def body(i, _):
            a, tile = i // 4, lax.rem(i, 4)
            s0 = pl.multiple_of(tile * 16, 16)
            for ip in range(16):
                zbuf[pl.ds(ip * 16, 16), :] = arrived[u, a, pl.ds(s0, 16), pl.ds(ip * 128, 128)].astype(F32)
            for s in range(16):
                xt[b, s0 + s, pl.ds(pl.multiple_of(a * 16, 16), 16), :] = zbuf[pl.ds(s, 16, stride=16), :].astype(BF16)
            return 0
        lax.fori_loop(0, 16, body, 0)

    def product(u, b, m):
        even, odd, dens = [], [], []
        for q in range(0, CAPM, 2):
            t0 = xt[b, tab_s[u, 0, m * CAPM + q]]
            t1 = xt[b, tab_s[u, 0, m * CAPM + q + 1]]
            even.append(jnp.concatenate([t0[:, :64], t1[:, :64]], axis=1))
            odd.append(jnp.concatenate([t0[:, 64:], t1[:, 64:]], axis=1))
            dens.append(occ[tab_s[u, 1, m * CAPM + q]])
            dens.append(occ[tab_s[u, 1, m * CAPM + q + 1]])
        left = jnp.concatenate([jnp.concatenate(even, axis=1), jnp.concatenate(odd, axis=1)], axis=0)
        right = jnp.concatenate(dens, axis=0)
        return jnp.dot(left, right, preferred_element_type=F32)

    def store_sum(h, m, value, first):
        for ii in range(2):
            for a in range(4):
                part = value[(ii * 4 + a) * 16:(ii * 4 + a + 1) * 16]
                if first:
                    sums[h, m, ii, a] = part
                else:
                    sums[h, m, ii, a] += part

    for h in range(2):
        own[h].wait()
        relayout(h, 0)

        def first_body(m, _, h=h):
            store_sum(h, m, product(h, 0, m), True)
            return 0
        lax.fori_loop(0, NMB, first_body, 0)

    for d in (1, 3):
        for h in range(2):
            u = d * 2 + h
            sends[(0 if d == 1 else 2) + h].wait_recv()
            relayout(u, 0)

            def next_body(m, _, h=h, u=u):
                store_sum(h, m, product(u, 0, m), False)
                return 0
            lax.fori_loop(0, NMB, next_body, 0)

    for h in range(2):
        sends[4 + h].wait_recv()
        relayout(4 + h, h)

    second = {}
    for t in range(4):
        mu0 = lax.rem(z + ORDER[t], 4) * 4
        for h in range(2):
            me = y if h == 0 else x

            def last_body(i, _, h=h, t=t, mu0=mu0, me=me):
                m = mu0 + i
                store_sum(h, m, product(4 + h, h, m), False)
                for d in range(1, 4):
                    for ii in range(2):
                        sbuf[h, d - 1, t, i, ii] = sums[h, m, ii, lax.rem(me + d, 4)].astype(BF16)
                return 0
            lax.fori_loop(0, 4, last_body, 0)
            for d in (2, 1, 3):
                copy = pltpu.make_async_remote_copy(
                    src_ref=sbuf.at[h, d - 1, t], dst_ref=rbuf.at[h, d - 1, t],
                    send_sem=s2.at[h, d - 1, t], recv_sem=r2.at[h, d - 1, t],
                    device_id=ring(1 - h, d), device_id_type=MESH)
                copy.start()
                second[t, h, d] = copy

    third = {}
    for t in range(4):
        zt = lax.rem(z + ORDER[t], 4)
        mu0 = zt * 4
        for h in range(2):
            for d in (1, 3, 2):
                second[t, h, d].wait_recv()
            me = y if h == 0 else x
            for i in range(4):
                for ii in range(2):
                    total = sums[h, mu0 + i, ii, me]
                    for d in range(3):
                        total = total + rbuf[h, d, t, i, ii].astype(F32)
                    hbuf[t, i // 2, pl.ds(((i % 2) * 4 + h * 2 + ii) * 16, 16), :] = total.astype(BF16)
        if t < 3:
            for k in range(2):
                copy = pltpu.make_async_remote_copy(
                    src_ref=hbuf.at[t, k], dst_ref=gbuf.at[row],
                    send_sem=s3.at[t, k], recv_sem=r3.at[t, core],
                    device_id=(zt * 2 + k, col), device_id_type=MESH)
                copy.start()
                third[t, k] = copy
        else:
            copy = pltpu.make_async_remote_copy(
                src_ref=hbuf.at[t, 1 - core], dst_ref=gbuf.at[row],
                send_sem=s3.at[t, 0], recv_sem=r3.at[t, 0],
                device_id=(z * 2 + 1 - core, col), device_id_type=MESH)
            copy.start()
            third[t, 0] = copy
            mine = pltpu.make_async_copy(hbuf.at[t, core], gbuf.at[row], loc_sem)
            mine.start()

    for t in range(4):
        if t < 3:
            for k in range(2):
                g = lax.rem(z + 4 - ORDER[t], 4) * 2 + k
                pltpu.make_async_remote_copy(
                    src_ref=hbuf.at[t, k], dst_ref=gbuf.at[g], send_sem=s3.at[t, k], recv_sem=r3.at[t, k],
                    device_id=(zt * 2 + k, col), device_id_type=MESH).wait_recv()
                o_ref[g] = jnp.dot(virt, gbuf[g], preferred_element_type=F32).astype(BF16)
        else:
            mine.wait()
            o_ref[row] = jnp.dot(virt, gbuf[row], preferred_element_type=F32).astype(BF16)
            third[t, 0].wait_recv()
            g = z * 2 + 1 - core
            o_ref[g] = jnp.dot(virt, gbuf[g], preferred_element_type=F32).astype(BF16)

    for copy in sends + list(second.values()) + list(third.values()):
        copy.wait_send()


def local(tensor, pair_mu, pair_nu, occ_density, virt_density):
    dma = pltpu.SemaphoreType.DMA
    out = pl.pallas_call(
        kernel,
        out_shape=jax.ShapeDtypeStruct((8, 128, NNU), BF16),
        in_specs=[
            pl.BlockSpec(memory_space=pl.ANY),
            pl.BlockSpec(memory_space=pltpu.VMEM),
            pl.BlockSpec(memory_space=pltpu.VMEM),
            pl.BlockSpec(memory_space=pl.ANY),
            pl.BlockSpec(memory_space=pltpu.VMEM),
        ],
        out_specs=pl.BlockSpec(memory_space=pltpu.VMEM),
        scratch_shapes=[
            pltpu.VMEM((8, 4, PAIRS, HALF), BF16),
            pltpu.VMEM((NBNU + 1, BS, NNU), BF16),
            pltpu.VMEM((256, 128), F32),
            pltpu.VMEM((2, PAIRS, 64, 128), BF16),
            pltpu.VMEM((2, NMB, 2, 4, 16, NNU), F32),
            pltpu.VMEM((2, 3, 4, 4, 2, 16, NNU), BF16),
            pltpu.VMEM((2, 3, 4, 4, 2, 16, NNU), BF16),
            pltpu.VMEM((4, 2, 128, NNU), BF16),
            pltpu.VMEM((8, 128, NNU), BF16),
            pltpu.VMEM((8, 128), jnp.int32),
            pltpu.VMEM((8, 8, 128), jnp.int32),
            pltpu.SMEM((8, 8, 128), jnp.int32),
            dma, dma((2,)), dma((8,)), dma((8,)), dma((8,)), dma((8,)), dma,
            dma((2, 3, 4)), dma((2, 3, 4)), dma((4, 2)), dma((4, 2)), dma,
        ],
        compiler_params=pltpu.CompilerParams(
            collective_id=0, has_side_effects=True, vmem_limit_bytes=56 << 20),
        name="density_transform",
    )(
        tensor.reshape(4, 4, PAIRS, BS * BS),
        pair_mu.reshape(1, PAIRS),
        pair_nu.reshape(1, PAIRS),
        occ_density.reshape(NBNU, BS, NNU),
        virt_density,
    )
    return out.reshape(8, 1, 128, NNU)


def solution(mesh):
    placed = (P("row", "col", None), P("col"), P("col"), P(), P("row", None))
    return jax.shard_map(
        local, mesh=mesh, in_specs=placed, out_specs=P(None, "col", "row", None), check_vma=False
    )
```

time: 857 us -> 119 us (0.14)
  blocking collectives: 539 us -> 0 us
  waiting for transfers between devices: 179 us -> 0 us
  Pallas kernels: 0 us -> 117 us
  local copies, waits for them, and re-layouts: 87.9 us -> 2.09 us
  matrix products: 21.6 us -> 0 us
  other arithmetic: 18.1 us -> 0 us
    unnamed x1 -> x0, blocking collectives: 539 us -> none
    all_to_all x1 -> x0, waiting for transfers between devices: 179 us -> none  [local(): lax.all_to_all(packed, 'row', split_axis=2, concat_axis=0, tiled=True)]
    pallas_call x0 -> x1, Pallas kernels: none -> 117 us  [local(): pl.pallas_call(kernel, out_shape=jax.ShapeDtypeStruct((8, 128, NNU), BF16...]
    reshape x5 -> x0, local copies, waits for them, and re-layouts: 46.3 us -> none  [the longest x1 46 us: local(): blocks_in = arrived.reshape(row_count, aux_rows, 2, CAPM, BS, BS)]
    gather x2 -> x0, local copies, waits for them, and re-layouts: 37.8 us -> none  [the longest x1 34.3 us: local(): picked = jnp.take(tensor, source.reshape(-1), axis=1)]
    dot_general x2 -> x0, matrix products: 21.6 us -> none  [the longest x1 21.2 us: local(): jnp.einsum('raqkij,qkjo->raqio', blocks_in, selected, preferred_element_t...]
    mul x1 -> x0, other arithmetic: 14.2 us -> none  [local(): picked = picked * filled.reshape(1, -1, 1).astype(picked.dtype)]
  transfers between devices with their start and end apart: 1 -> 0, of which waited for: 1 -> 0; matrix products, arithmetic and copies ran while one was open for 1% -> 0% of each run, Pallas kernels for 0% -> 0%
where the time goes in v1:
time: 119 us
  Pallas kernels  117 us (98%)
  local copies, waits for them, and re-layouts  2.09 us (2%)
    pallas_call x1, Pallas kernels, local(): pl.pallas_call(kernel, out_shape=jax.ShapeDtypeStruct((8, 128, NNU), BF16...  117 us

profile of v1, /device:TPU:1, one launch (start us, length us, event | category | flops | bytes accessed | tf_op | source)
XLA Modules:
  0.0 119.0 jit_solution(16533447458258973740)
XLA Ops:
  0.0 116.9 %density_transform.1 = bf16[8,128,384]{2,1,0:T(8,128)(2,1)} custom-call(bf16[4,4,64,4096]{3,2,1,0:T(8,128)(2,1)} %bitcast.7, s32[1,64]{1,0:T(1,128)} %bitcast.10, s32[1,64]{1,0:T(1,128)} %bitcast.11, bf16[128,64,384]{2,1,0:T(8,128)(2,1)} %bitcast.8, bf16[128,128]{1,0:T(8,128)(2,1)} %virt_ref.1), custom_call_target="tpu_custom_call" | custom-call | tf_op jit(solution)/shard_map/density_transform/pallas_call | solution.py:241
  116.9 2.1 %copy.8 = bf16[8,1,128,384]{3,2,1,0:T(8,128)(2,1)} copy(bf16[8,1,128,384]{3,2,1,0:T(8,128)(2,1)} %bitcast.9) | data formatting | bytes 1572864

commit v2 on v1

v2 whole, which is shorter than its diff:
```python
import jax
import jax.numpy as jnp
from jax import lax
from jax.experimental import pallas as pl
from jax.experimental.pallas import tpu as pltpu
from jax.sharding import PartitionSpec as P

MESH = pl.DeviceIdType.MESH
BS = 64
NNU = 384
NBNU = 128
NMB = 16
CAPM = 8
PAIRS = 64
HALF = 2048
F32 = jnp.float32
BF16 = jnp.bfloat16


def slot_table(mu_row, nu_row):
    sub = lax.broadcasted_iota(jnp.int32, (PAIRS, PAIRS), 0)
    lane = lax.broadcasted_iota(jnp.int32, (PAIRS, PAIRS), 1)
    mu_b = jnp.broadcast_to(mu_row, (PAIRS, PAIRS))
    nu_b = jnp.broadcast_to(nu_row, (PAIRS, PAIRS))
    mu_col = jnp.sum(jnp.where(sub == lane, mu_b, 0), axis=1, keepdims=True)
    nu_col = jnp.sum(jnp.where(sub == lane, nu_b, 0), axis=1, keepdims=True)
    rank = jnp.sum(jnp.where((mu_b == mu_col) & (lane < sub), 1, 0), axis=1, keepdims=True)
    slot = lax.broadcasted_iota(jnp.int32, (PAIRS, NMB * CAPM), 1)
    pair = lax.broadcasted_iota(jnp.int32, (PAIRS, NMB * CAPM), 0)
    hit = (mu_col * CAPM + rank) == slot
    source = jnp.sum(jnp.where(hit, pair, 0), axis=0, keepdims=True)
    target = jnp.sum(jnp.where(hit, nu_col - NBNU, 0), axis=0, keepdims=True) + NBNU
    row = lax.broadcasted_iota(jnp.int32, (8, NMB * CAPM), 0)
    return jnp.where(row == 0, source, target)


def kernel(t_ref, mu_ref, nu_ref, occ_ref, virt_ref, o_ref,
           own, arr_c, arr_d, occ, xown, xt, sums, csums, cbuf, crecv, tbuf, sbuf, rbuf, hbuf, gbuf, tab_v, tab_r, tab_s,
           occ_sem, own_sem, sc, rc, sd, rd, st, rt, tab_sem, sp, rp, s2, r2, s3, r3, loc_sem):
    row, col = lax.axis_index("row"), lax.axis_index("col")
    x, y, z, core = col // 4, col % 4, row // 2, row % 2

    def at_x(d):
        return (row, lax.rem(x + d, 4) * 4 + y)

    def at_y(d):
        return (row, x * 4 + lax.rem(y + d, 4))

    def ring(h, d):
        return at_x(d) if h == 0 else at_y(d)

    def place(h):
        return x if h == 0 else y

    def piece(h, d, first, count):
        if h == 0:
            return t_ref.at[lax.rem(x + d, 4), pl.ds(first, count), :, pl.ds(0, HALF)]
        return t_ref.at[pl.ds(first, count), lax.rem(y + d, 4), :, pl.ds(HALF, HALF)]

    locals_ = []
    for h in range(2):
        for k, (d, first, count, at) in enumerate(((0, 0, 4, 0), (1, 0, 2, 4), (3, 2, 2, 6))):
            copy = pltpu.make_async_copy(piece(h, d, first, count), own.at[h, pl.ds(at, count)], own_sem.at[h, k])
            copy.start()
            locals_.append(copy)
    occ_copy = pltpu.make_async_copy(occ_ref, occ.at[pl.ds(0, NBNU)], occ_sem)
    occ_copy.start()

    barrier = pltpu.get_barrier_semaphore()
    for d in range(1, 4):
        pl.semaphore_signal(barrier, inc=1, device_id=at_x(d), device_id_type=MESH)
        pl.semaphore_signal(barrier, inc=1, device_id=at_y(d), device_id_type=MESH)
    for d in range(1, 8):
        pl.semaphore_signal(barrier, inc=1, device_id=(lax.rem(row + d, 8), col), device_id_type=MESH)
    pl.semaphore_wait(barrier, 13)

    cs, ds, tabs = {}, {}, {}
    for w in range(2):
        for h in range(2):
            cs[h, w] = pltpu.make_async_remote_copy(
                src_ref=piece(h, 2, 2 * w, 2), dst_ref=arr_c.at[h * 2 + w], send_sem=sc.at[h, w], recv_sem=rc.at[h, w],
                device_id=ring(h, 1 + 2 * w), device_id_type=MESH)
            ds[h, w] = pltpu.make_async_remote_copy(
                src_ref=piece(h, 1 + 2 * w, 2 - 2 * w, 2), dst_ref=arr_d.at[h * 2 + w], send_sem=sd.at[h, w], recv_sem=rd.at[h, w],
                device_id=ring(h, 1 + 2 * w), device_id_type=MESH)
            cs[h, w].start()

    tab_v[...] = slot_table(mu_ref[...], nu_ref[...])
    tab_r[4] = tab_v[...]
    for w in range(2):
        for h in range(2):
            copy = pltpu.make_async_remote_copy(
                src_ref=tab_v, dst_ref=tab_r.at[h * 2 + w], send_sem=st.at[h, w], recv_sem=rt.at[h, w],
                device_id=ring(h, 1 + 2 * w), device_id_type=MESH)
            copy.start()
            tabs[h, w] = copy
    occ[NBNU] = jnp.zeros((BS, NNU), BF16)
    c = lax.broadcasted_iota(jnp.int32, (128, 128), 1)
    r = lax.broadcasted_iota(jnp.int32, (128, 128), 0)
    from_col = (c // 64) * 64 + ((c // 32) % 2) * 32 + (c % 16) * 2 + (c // 16) % 2
    perm = jnp.where(r == from_col, 1.0, 0.0).astype(BF16)
    virt = jnp.dot(virt_ref[...], perm, preferred_element_type=F32).astype(BF16)

    def relayout(src, dst, aux_count):
        def body(i, _):
            a, s0 = i // 4, pl.multiple_of(lax.rem(i, 4) * 16, 16)
            dst[pl.ds(s0, 16), pl.ds(pl.multiple_of(a * 16, 16), 16), :] = src[a, pl.ds(s0, 16), :].reshape(16, 16, 128)
            return 0
        lax.fori_loop(0, aux_count * 4, body, 0, unroll=2)

    for copy in locals_:
        copy.wait()
    for h in range(2):
        relayout(own.at[h], xown.at[h], 8)
    for copy in tabs.values():
        copy.wait_recv()
    tab_copy = pltpu.make_async_copy(tab_r, tab_s, tab_sem)
    tab_copy.start()
    tab_copy.wait()
    occ_copy.wait()

    def product(blocks, k, m):
        even, odd, dens = [], [], []
        for q in range(0, CAPM, 2):
            t0 = blocks[tab_s[k, 0, m * CAPM + q]]
            t1 = blocks[tab_s[k, 0, m * CAPM + q + 1]]
            even.append(jnp.concatenate([t0[:, :64], t1[:, :64]], axis=1))
            odd.append(jnp.concatenate([t0[:, 64:], t1[:, 64:]], axis=1))
            dens.append(occ[tab_s[k, 1, m * CAPM + q]])
            dens.append(occ[tab_s[k, 1, m * CAPM + q + 1]])
        left = jnp.concatenate([jnp.concatenate(even, axis=1), jnp.concatenate(odd, axis=1)], axis=0)
        right = jnp.concatenate(dens, axis=0)
        return jnp.dot(left, right, preferred_element_type=F32)

    def own_body(m, _):
        for h in range(2):
            value = product(xown.at[h], 4, m).reshape(2, 8, 16, NNU)
            sums[h, m] = value[:, 0:4]
            csums[h * 2, m] = value[:, 4:6]
            csums[h * 2 + 1, m] = value[:, 6:8]
        return 0
    lax.fori_loop(0, NMB, own_body, 0, unroll=2)

    for copy in cs.values():
        copy.wait_send()
    for copy in ds.values():
        copy.start()
    for u in range(4):
        cs[u // 2, u % 2].wait_recv()
        relayout(arr_c.at[u], xt.at[u], 2)

    def pair_copy(u, t):
        return pltpu.make_async_remote_copy(
            src_ref=cbuf.at[u, t], dst_ref=crecv.at[u, t], send_sem=sp.at[u, t], recv_sem=rp.at[u, t],
            device_id=ring(u // 2, 1 + 2 * (u % 2)), device_id_type=MESH)

    def c_body(t, _):
        mu0 = lax.rem(z + t + 1, 4) * 4
        for u in range(4):
            for i in range(4):
                value = product(xt.at[u], u, mu0 + i).reshape(2, 2, 16, NNU)
                cbuf[u, t, i] = (value + csums[u, mu0 + i]).astype(BF16)
        for u in range(4):
            pair_copy(u, t).start()
        return 0
    lax.fori_loop(0, 4, c_body, 0)

    for u in range(4):
        ds[u // 2, u % 2].wait_recv()
        relayout(arr_d.at[u], xt.at[u], 2)

    def d_body(m, _):
        for u in range(4):
            h, w = u // 2, u % 2
            value = product(xt.at[u], u, m).reshape(2, 2, 16, NNU)
            sums[h, m, :, pl.ds(2 - 2 * w, 2)] += value
        return 0
    lax.fori_loop(0, NMB, d_body, 0, unroll=2)

    def second(h, d, t):
        return pltpu.make_async_remote_copy(
            src_ref=sbuf.at[h, d - 1, t], dst_ref=rbuf.at[h, d - 1, t],
            send_sem=s2.at[h, d - 1, t], recv_sem=r2.at[h, d - 1, t],
            device_id=ring(1 - h, d), device_id_type=MESH)

    def p2_body(t, _):
        mu0 = lax.rem(z + t + 1, 4) * 4
        for h in range(2):
            for w in range(2):
                pair_copy(h * 2 + w, t).wait_recv()
            for d in (2, 1, 3, 0):
                a = lax.rem(place(1 - h) + d, 4)
                for i in range(4):
                    for ii in range(2):
                        total = sums[h, mu0 + i, ii, a] + crecv[h * 2 + a // 2, t, i, ii, lax.rem(a, 2)].astype(F32)
                        if d == 0:
                            tbuf[h, t, i, ii] = total
                        else:
                            sbuf[h, d - 1, t, i, ii] = total.astype(BF16)
                if d > 0:
                    second(h, d, t).start()
        return 0
    lax.fori_loop(0, 4, p2_body, 0)

    def third(t, k):
        return pltpu.make_async_remote_copy(
            src_ref=hbuf.at[t, k], dst_ref=gbuf.at[row],
            send_sem=s3.at[t, k], recv_sem=r3.at[t, core],
            device_id=(lax.rem(z + t + 1, 4) * 2 + k, col), device_id_type=MESH)

    across = pltpu.make_async_remote_copy(
        src_ref=hbuf.at[3, 1 - core], dst_ref=gbuf.at[row],
        send_sem=s3.at[3, 0], recv_sem=r3.at[3, 0],
        device_id=(z * 2 + 1 - core, col), device_id_type=MESH)
    mine = pltpu.make_async_copy(hbuf.at[3, core], gbuf.at[row], loc_sem)

    def finish(t):
        for h in range(2):
            for d in (1, 3, 2):
                second(h, d, t).wait_recv()
            for i in range(4):
                for ii in range(2):
                    total = tbuf[h, t, i, ii]
                    for d in range(3):
                        total = total + rbuf[h, d, t, i, ii].astype(F32)
                    hbuf[t, i // 2, pl.ds(((i % 2) * 4 + h * 2 + ii) * 16, 16), :] = total.astype(BF16)

    def p3_body(t, _):
        finish(t)
        for k in range(2):
            third(t, k).start()
        return 0
    lax.fori_loop(0, 3, p3_body, 0)
    finish(3)
    across.start()
    mine.start()

    def last_body(t, _):
        for k in range(2):
            g = lax.rem(z + 3 - t, 4) * 2 + k
            pltpu.make_async_remote_copy(
                src_ref=hbuf.at[t, k], dst_ref=gbuf.at[g], send_sem=s3.at[t, k], recv_sem=r3.at[t, k],
                device_id=(row, col), device_id_type=MESH).wait_recv()
            o_ref[g] = jnp.dot(virt, gbuf[g], preferred_element_type=F32).astype(BF16)
        return 0
    lax.fori_loop(0, 3, last_body, 0)
    mine.wait()
    o_ref[row] = jnp.dot(virt, gbuf[row], preferred_element_type=F32).astype(BF16)
    across.wait_recv()
    other = z * 2 + 1 - core
    o_ref[other] = jnp.dot(virt, gbuf[other], preferred_element_type=F32).astype(BF16)

    across.wait_send()
    for copy in [*ds.values(), *tabs.values()]:
        copy.wait_send()

    def sent_body(t, _):
        for u in range(4):
            pair_copy(u, t).wait_send()
        for h in range(2):
            for d in range(1, 4):
                second(h, d, t).wait_send()
        return 0
    lax.fori_loop(0, 4, sent_body, 0)
    for t in range(3):
        for k in range(2):
            third(t, k).wait_send()


def local(tensor, pair_mu, pair_nu, occ_density, virt_density):
    dma = pltpu.SemaphoreType.DMA
    out = pl.pallas_call(
        kernel,
        out_shape=jax.ShapeDtypeStruct((8, 128, NNU), BF16),
        in_specs=[
            pl.BlockSpec(memory_space=pl.ANY),
            pl.BlockSpec(memory_space=pltpu.VMEM),
            pl.BlockSpec(memory_space=pltpu.VMEM),
            pl.BlockSpec(memory_space=pl.ANY),
            pl.BlockSpec(memory_space=pltpu.VMEM),
        ],
        out_specs=pl.BlockSpec(memory_space=pltpu.VMEM),
        scratch_shapes=[
            pltpu.VMEM((2, 8, PAIRS, HALF), BF16),
            pltpu.VMEM((4, 2, PAIRS, HALF), BF16),
            pltpu.VMEM((4, 2, PAIRS, HALF), BF16),
            pltpu.VMEM((NBNU + 1, BS, NNU), BF16),
            pltpu.VMEM((2, PAIRS, 128, 128), BF16),
            pltpu.VMEM((4, PAIRS, 32, 128), BF16),
            pltpu.VMEM((2, NMB, 2, 4, 16, NNU), F32),
            pltpu.VMEM((4, NMB, 2, 2, 16, NNU), F32),
            pltpu.VMEM((4, 4, 4, 2, 2, 16, NNU), BF16),
            pltpu.VMEM((4, 4, 4, 2, 2, 16, NNU), BF16),
            pltpu.VMEM((2, 4, 4, 2, 16, NNU), F32),
            pltpu.VMEM((2, 3, 4, 4, 2, 16, NNU), BF16),
            pltpu.VMEM((2, 3, 4, 4, 2, 16, NNU), BF16),
            pltpu.VMEM((4, 2, 128, NNU), BF16),
            pltpu.VMEM((8, 128, NNU), BF16),
            pltpu.VMEM((8, 128), jnp.int32),
            pltpu.VMEM((5, 8, 128), jnp.int32),
            pltpu.SMEM((5, 8, 128), jnp.int32),
            dma, dma((2, 3)), dma((2, 2)), dma((2, 2)), dma((2, 2)), dma((2, 2)), dma((2, 2)), dma((2, 2)), dma,
            dma((4, 4)), dma((4, 4)), dma((2, 3, 4)), dma((2, 3, 4)), dma((4, 2)), dma((4, 2)), dma,
        ],
        compiler_params=pltpu.CompilerParams(
            collective_id=0, has_side_effects=True, vmem_limit_bytes=60 << 20),
        name="density_transform",
    )(
        tensor.reshape(4, 4, PAIRS, BS * BS),
        pair_mu.reshape(1, PAIRS),
        pair_nu.reshape(1, PAIRS),
        occ_density.reshape(NBNU, BS, NNU),
        virt_density,
    )
    return out.reshape(8, 1, 128, NNU)


def solution(mesh):
    placed = (P("row", "col", None), P("col"), P("col"), P(), P("row", None))
    return jax.shard_map(
        local, mesh=mesh, in_specs=placed, out_specs=P(None, "col", "row", None), check_vma=False
    )
```

time: 119 us -> 85.1 us (0.72)
  Pallas kernels: 117 us -> 82.8 us
    pallas_call x1, Pallas kernels: 117 us -> 82.8 us  [local(): pl.pallas_call(kernel, out_shape=jax.ShapeDtypeStruct((8, 128, NNU), BF16...]
where the time goes in v2:
time: 85.1 us; the launch traced here: 84.9 us
  Pallas kernels  82.8 us (97%)
  local copies, waits for them, and re-layouts  2.09 us (2%)
    pallas_call x1, Pallas kernels, local(): pl.pallas_call(kernel, out_shape=jax.ShapeDtypeStruct((8, 128, NNU), BF16...  82.8 us
    unnamed x1, local copies, waits for them, and re-layouts  2.09 us

profile of v2, /device:TPU:1, one launch (start us, length us, event | category | flops | bytes accessed | tf_op | source)
XLA Modules:
  0.0 84.9 jit_solution(542203617485564093)
XLA Ops:
  0.0 82.8 %density_transform.1 = bf16[8,128,384]{2,1,0:T(8,128)(2,1)} custom-call(bf16[4,4,64,4096]{3,2,1,0:T(8,128)(2,1)} %bitcast.7, s32[1,64]{1,0:T(1,128)} %bitcast.10, s32[1,64]{1,0:T(1,128)} %bitcast.11, bf16[128,64,384]{2,1,0:T(8,128)(2,1)} %bitcast.8, bf16[128,128]{1,0:T(8,128)(2,1)} %virt_ref.1), custom_call_target="tpu_custom_call" | custom-call | tf_op jit(solution)/shard_map/density_transform/pallas_call | solution.py:272
  82.8 2.1 %copy.8 = bf16[8,1,128,384]{3,2,1,0:T(8,128)(2,1)} copy(bf16[8,1,128,384]{3,2,1,0:T(8,128)(2,1)} %bitcast.9) | data formatting | bytes 1572864

commit v3 on v2

--- a/solution.py
+++ b/solution.py
@@ -12,6 +12,10 @@
 NMB = 16
 CAPM = 8
 PAIRS = 64
+CHUNKS = 8
+EARLY = 1
+AHEAD = 2
+LAG = 2
 HALF = 2048
 F32 = jnp.float32
 BF16 = jnp.bfloat16
@@ -36,7 +40,7 @@
 
 def kernel(t_ref, mu_ref, nu_ref, occ_ref, virt_ref, o_ref,
            own, arr_c, arr_d, occ, xown, xt, sums, csums, cbuf, crecv, tbuf, sbuf, rbuf, hbuf, gbuf, tab_v, tab_r, tab_s,
-           occ_sem, own_sem, sc, rc, sd, rd, st, rt, tab_sem, sp, rp, s2, r2, s3, r3, loc_sem):
+           occ_sem, own_sem, sc, rc, sd, rd, st, rt, tab_sem, sp, rp, s2, r2, s3, r3):
     row, col = lax.axis_index("row"), lax.axis_index("col")
     x, y, z, core = col // 4, col % 4, row // 2, row % 2
 
@@ -139,43 +143,55 @@
             csums[h * 2, m] = value[:, 4:6]
             csums[h * 2 + 1, m] = value[:, 6:8]
         return 0
-    lax.fori_loop(0, NMB, own_body, 0, unroll=2)
-
+    lax.fori_loop(0, 4, own_body, 0, unroll=2)
     for copy in cs.values():
         copy.wait_send()
     for copy in ds.values():
         copy.start()
+    lax.fori_loop(4, NMB, own_body, 0, unroll=2)
+
     for u in range(4):
         cs[u // 2, u % 2].wait_recv()
         relayout(arr_c.at[u], xt.at[u], 2)
+
+    def chunk_row(t):
+        return lax.rem(z + t // 2 + 1, 4) * 2 + lax.rem(t + 1 + core, 2)
 
     def pair_copy(u, t):
         return pltpu.make_async_remote_copy(
             src_ref=cbuf.at[u, t], dst_ref=crecv.at[u, t], send_sem=sp.at[u, t], recv_sem=rp.at[u, t],
             device_id=ring(u // 2, 1 + 2 * (u % 2)), device_id_type=MESH)
 
+    def start_pair(t):
+        for u in range(4):
+            pair_copy(u, t).start()
+
     def c_body(t, _):
-        mu0 = lax.rem(z + t + 1, 4) * 4
+        mu0 = chunk_row(t) * 2
         for u in range(4):
-            for i in range(4):
+            for i in range(2):
                 value = product(xt.at[u], u, mu0 + i).reshape(2, 2, 16, NNU)
                 cbuf[u, t, i] = (value + csums[u, mu0 + i]).astype(BF16)
-        for u in range(4):
-            pair_copy(u, t).start()
-        return 0
-    lax.fori_loop(0, 4, c_body, 0)
-
+
+        @pl.when(t < EARLY)
+        def _():
+            start_pair(t)
+        return 0
+    lax.fori_loop(0, CHUNKS, c_body, 0)
+
+    for copy in ds.values():
+        copy.wait_send()
+    for t in range(EARLY, AHEAD):
+        start_pair(t)
     for u in range(4):
         ds[u // 2, u % 2].wait_recv()
         relayout(arr_d.at[u], xt.at[u], 2)
 
-    def d_body(m, _):
+    def direct(m):
         for u in range(4):
             h, w = u // 2, u % 2
             value = product(xt.at[u], u, m).reshape(2, 2, 16, NNU)
             sums[h, m, :, pl.ds(2 - 2 * w, 2)] += value
-        return 0
-    lax.fori_loop(0, NMB, d_body, 0, unroll=2)
 
     def second(h, d, t):
         return pltpu.make_async_remote_copy(
@@ -183,14 +199,32 @@
             send_sem=s2.at[h, d - 1, t], recv_sem=r2.at[h, d - 1, t],
             device_id=ring(1 - h, d), device_id_type=MESH)
 
-    def p2_body(t, _):
-        mu0 = lax.rem(z + t + 1, 4) * 4
+    def third(t):
+        return pltpu.make_async_remote_copy(
+            src_ref=hbuf.at[t], dst_ref=gbuf.at[row], send_sem=s3.at[t], recv_sem=r3.at[t],
+            device_id=(chunk_row(t), col), device_id_type=MESH)
+
+    def finish(t):
+        for h in range(2):
+            for d in (1, 3, 2):
+                second(h, d, t).wait_recv()
+            for i in range(2):
+                for ii in range(2):
+                    total = tbuf[h, t, i, ii]
+                    for d in range(3):
+                        total = total + rbuf[h, d, t, i, ii].astype(F32)
+                    hbuf[t, pl.ds((i * 4 + h * 2 + ii) * 16, 16), :] = total.astype(BF16)
+
+    def chunk(t, _):
+        mu0 = chunk_row(t) * 2
+        for i in range(2):
+            direct(mu0 + i)
         for h in range(2):
             for w in range(2):
                 pair_copy(h * 2 + w, t).wait_recv()
             for d in (2, 1, 3, 0):
                 a = lax.rem(place(1 - h) + d, 4)
-                for i in range(4):
+                for i in range(2):
                     for ii in range(2):
                         total = sums[h, mu0 + i, ii, a] + crecv[h * 2 + a // 2, t, i, ii, lax.rem(a, 2)].astype(F32)
                         if d == 0:
@@ -199,59 +233,35 @@
                             sbuf[h, d - 1, t, i, ii] = total.astype(BF16)
                 if d > 0:
                     second(h, d, t).start()
-        return 0
-    lax.fori_loop(0, 4, p2_body, 0)
-
-    def third(t, k):
-        return pltpu.make_async_remote_copy(
-            src_ref=hbuf.at[t, k], dst_ref=gbuf.at[row],
-            send_sem=s3.at[t, k], recv_sem=r3.at[t, core],
-            device_id=(lax.rem(z + t + 1, 4) * 2 + k, col), device_id_type=MESH)
-
-    across = pltpu.make_async_remote_copy(
-        src_ref=hbuf.at[3, 1 - core], dst_ref=gbuf.at[row],
-        send_sem=s3.at[3, 0], recv_sem=r3.at[3, 0],
-        device_id=(z * 2 + 1 - core, col), device_id_type=MESH)
-    mine = pltpu.make_async_copy(hbuf.at[3, core], gbuf.at[row], loc_sem)
-
-    def finish(t):
-        for h in range(2):
-            for d in (1, 3, 2):
-                second(h, d, t).wait_recv()
-            for i in range(4):
-                for ii in range(2):
-                    total = tbuf[h, t, i, ii]
-                    for d in range(3):
-                        total = total + rbuf[h, d, t, i, ii].astype(F32)
-                    hbuf[t, i // 2, pl.ds(((i % 2) * 4 + h * 2 + ii) * 16, 16), :] = total.astype(BF16)
-
-    def p3_body(t, _):
+
+        @pl.when(t < CHUNKS - AHEAD)
+        def _():
+            start_pair(t + AHEAD)
+
+        @pl.when(t >= LAG)
+        def _():
+            finish(t - LAG)
+            third(t - LAG).start()
+        return 0
+    lax.fori_loop(0, CHUNKS, chunk, 0)
+
+    for t in range(CHUNKS - LAG, 7):
         finish(t)
-        for k in range(2):
-            third(t, k).start()
-        return 0
-    lax.fori_loop(0, 3, p3_body, 0)
-    finish(3)
-    across.start()
-    mine.start()
+        third(t).start()
 
     def last_body(t, _):
-        for k in range(2):
-            g = lax.rem(z + 3 - t, 4) * 2 + k
-            pltpu.make_async_remote_copy(
-                src_ref=hbuf.at[t, k], dst_ref=gbuf.at[g], send_sem=s3.at[t, k], recv_sem=r3.at[t, k],
-                device_id=(row, col), device_id_type=MESH).wait_recv()
-            o_ref[g] = jnp.dot(virt, gbuf[g], preferred_element_type=F32).astype(BF16)
-        return 0
-    lax.fori_loop(0, 3, last_body, 0)
-    mine.wait()
-    o_ref[row] = jnp.dot(virt, gbuf[row], preferred_element_type=F32).astype(BF16)
-    across.wait_recv()
-    other = z * 2 + 1 - core
-    o_ref[other] = jnp.dot(virt, gbuf[other], preferred_element_type=F32).astype(BF16)
-
-    across.wait_send()
-    for copy in [*ds.values(), *tabs.values()]:
+        g = lax.rem(z + 3 - t // 2, 4) * 2 + lax.rem(t + 1 + core, 2)
+        pltpu.make_async_remote_copy(
+            src_ref=hbuf.at[t], dst_ref=gbuf.at[g], send_sem=s3.at[t], recv_sem=r3.at[t],
+            device_id=(row, col), device_id_type=MESH).wait_recv()
+        o_ref[g] = jnp.dot(virt, gbuf[g], preferred_element_type=F32).astype(BF16)
+        return 0
+    lax.fori_loop(0, 6, last_body, 0)
+    finish(7)
+    o_ref[row] = jnp.dot(virt, hbuf[7], preferred_element_type=F32).astype(BF16)
+    last_body(6, 0)
+
+    for copy in tabs.values():
         copy.wait_send()
 
     def sent_body(t, _):
@@ -260,11 +270,12 @@
         for h in range(2):
             for d in range(1, 4):
                 second(h, d, t).wait_send()
-        return 0
-    lax.fori_loop(0, 4, sent_body, 0)
-    for t in range(3):
-        for k in range(2):
-            third(t, k).wait_send()
+
+        @pl.when(t < 7)
+        def _():
+            third(t).wait_send()
+        return 0
+    lax.fori_loop(0, CHUNKS, sent_body, 0)
 
 
 def local(tensor, pair_mu, pair_nu, occ_density, virt_density):
@@ -289,18 +300,18 @@
             pltpu.VMEM((4, PAIRS, 32, 128), BF16),
             pltpu.VMEM((2, NMB, 2, 4, 16, NNU), F32),
             pltpu.VMEM((4, NMB, 2, 2, 16, NNU), F32),
-            pltpu.VMEM((4, 4, 4, 2, 2, 16, NNU), BF16),
-            pltpu.VMEM((4, 4, 4, 2, 2, 16, NNU), BF16),
-            pltpu.VMEM((2, 4, 4, 2, 16, NNU), F32),
-            pltpu.VMEM((2, 3, 4, 4, 2, 16, NNU), BF16),
-            pltpu.VMEM((2, 3, 4, 4, 2, 16, NNU), BF16),
-            pltpu.VMEM((4, 2, 128, NNU), BF16),
+            pltpu.VMEM((4, CHUNKS, 2, 2, 2, 16, NNU), BF16),
+            pltpu.VMEM((4, CHUNKS, 2, 2, 2, 16, NNU), BF16),
+            pltpu.VMEM((2, CHUNKS, 2, 2, 16, NNU), F32),
+            pltpu.VMEM((2, 3, CHUNKS, 2, 2, 16, NNU), BF16),
+            pltpu.VMEM((2, 3, CHUNKS, 2, 2, 16, NNU), BF16),
+            pltpu.VMEM((8, 128, NNU), BF16),
             pltpu.VMEM((8, 128, NNU), BF16),
             pltpu.VMEM((8, 128), jnp.int32),
             pltpu.VMEM((5, 8, 128), jnp.int32),
             pltpu.SMEM((5, 8, 128), jnp.int32),
             dma, dma((2, 3)), dma((2, 2)), dma((2, 2)), dma((2, 2)), dma((2, 2)), dma((2, 2)), dma((2, 2)), dma,
-            dma((4, 4)), dma((4, 4)), dma((2, 3, 4)), dma((2, 3, 4)), dma((4, 2)), dma((4, 2)), dma,
+            dma((4, CHUNKS)), dma((4, CHUNKS)), dma((2, 3, CHUNKS)), dma((2, 3, CHUNKS)), dma((7,)), dma((7,)),
         ],
         compiler_params=pltpu.CompilerParams(
             collective_id=0, has_side_effects=True, vmem_limit_bytes=60 << 20),

time: 85.1 us -> 78.1 us (0.918)
  Pallas kernels: 82.8 us -> 75.5 us
    pallas_call x1, Pallas kernels: 82.8 us -> 75.5 us  [local(): pl.pallas_call(kernel, out_shape=jax.ShapeDtypeStruct((8, 128, NNU), BF16...]
where the time goes in v3:
time: 78.1 us; the launch traced here: 77.7 us
  Pallas kernels  75.5 us (97%)
  local copies, waits for them, and re-layouts  2.09 us (3%)
    pallas_call x1, Pallas kernels, local(): pl.pallas_call(kernel, out_shape=jax.ShapeDtypeStruct((8, 128, NNU), BF16...  75.5 us
    unnamed x1, local copies, waits for them, and re-layouts  2.09 us

profile of v3, /device:TPU:1, one launch (start us, length us, event | category | flops | bytes accessed | tf_op | source)
XLA Modules:
  0.0 77.7 jit_solution(4948620485475335239)
XLA Ops:
  0.0 75.5 %density_transform.1 = bf16[8,128,384]{2,1,0:T(8,128)(2,1)} custom-call(bf16[4,4,64,4096]{3,2,1,0:T(8,128)(2,1)} %bitcast.7, s32[1,64]{1,0:T(1,128)} %bitcast.10, s32[1,64]{1,0:T(1,128)} %bitcast.11, bf16[128,64,384]{2,1,0:T(8,128)(2,1)} %bitcast.8, bf16[128,128]{1,0:T(8,128)(2,1)} %virt_ref.1), custom_call_target="tpu_custom_call" | custom-call | tf_op jit(solution)/shard_map/density_transform/pallas_call | solution.py:283
  75.6 2.1 %copy.8 = bf16[8,1,128,384]{3,2,1,0:T(8,128)(2,1)} copy(bf16[8,1,128,384]{3,2,1,0:T(8,128)(2,1)} %bitcast.9) | data formatting | bytes 1572864

commit v4 on v3

--- a/solution.py
+++ b/solution.py
@@ -13,9 +13,9 @@
 CAPM = 8
 PAIRS = 64
 CHUNKS = 8
-EARLY = 1
-AHEAD = 2
-LAG = 2
+EARLY = 3
+AHEAD = 4
+LAG = 3
 HALF = 2048
 F32 = jnp.float32
 BF16 = jnp.bfloat16
@@ -39,8 +39,8 @@
 
 
 def kernel(t_ref, mu_ref, nu_ref, occ_ref, virt_ref, o_ref,
-           own, arr_c, arr_d, occ, xown, xt, sums, csums, cbuf, crecv, tbuf, sbuf, rbuf, hbuf, gbuf, tab_v, tab_r, tab_s,
-           occ_sem, own_sem, sc, rc, sd, rd, st, rt, tab_sem, sp, rp, s2, r2, s3, r3):
+           own, arr_c, arr_d, occ, xown, xt, sums, csums, cbuf, crecv, tbuf, sbuf, rbuf, keep, gown, grecv, hbuf, gbuf, tab_v, tab_r, tab_s,
+           occ_sem, own_sem, sc, rc, sd, rd, st, rt, tab_sem, sp, rp, s2, r2, sg, rg, s3, r3):
     row, col = lax.axis_index("row"), lax.axis_index("col")
     x, y, z, core = col // 4, col % 4, row // 2, row % 2
 
@@ -116,6 +116,8 @@
         copy.wait()
     for h in range(2):
         relayout(own.at[h], xown.at[h], 8)
+    for copy in ds.values():
+        copy.start()
     for copy in tabs.values():
         copy.wait_recv()
     tab_copy = pltpu.make_async_copy(tab_r, tab_s, tab_sem)
@@ -144,10 +146,6 @@
             csums[h * 2 + 1, m] = value[:, 6:8]
         return 0
     lax.fori_loop(0, 4, own_body, 0, unroll=2)
-    for copy in cs.values():
-        copy.wait_send()
-    for copy in ds.values():
-        copy.start()
     lax.fori_loop(4, NMB, own_body, 0, unroll=2)
 
     for u in range(4):
@@ -193,27 +191,35 @@
             value = product(xt.at[u], u, m).reshape(2, 2, 16, NNU)
             sums[h, m, :, pl.ds(2 - 2 * w, 2)] += value
 
-    def second(h, d, t):
+    def outer(h, w, t):
         return pltpu.make_async_remote_copy(
-            src_ref=sbuf.at[h, d - 1, t], dst_ref=rbuf.at[h, d - 1, t],
-            send_sem=s2.at[h, d - 1, t], recv_sem=r2.at[h, d - 1, t],
-            device_id=ring(1 - h, d), device_id_type=MESH)
+            src_ref=sbuf.at[h, w, t], dst_ref=rbuf.at[h, w, t], send_sem=s2.at[h, w, t], recv_sem=r2.at[h, w, t],
+            device_id=ring(1 - h, 1 + 2 * w), device_id_type=MESH)
+
+    def inner(h, w, t):
+        return pltpu.make_async_remote_copy(
+            src_ref=gown.at[h, w, t], dst_ref=grecv.at[h, w, t], send_sem=sg.at[h, w, t], recv_sem=rg.at[h, w, t],
+            device_id=ring(1 - h, 1 + 2 * w), device_id_type=MESH)
 
     def third(t):
         return pltpu.make_async_remote_copy(
             src_ref=hbuf.at[t], dst_ref=gbuf.at[row], send_sem=s3.at[t], recv_sem=r3.at[t],
             device_id=(chunk_row(t), col), device_id_type=MESH)
 
+    def forward(t):
+        for h in range(2):
+            for w in range(2):
+                outer(h, w, t).wait_recv()
+                gown[h, w, t] = (keep[h, w, t] + rbuf[h, w, t, 0].astype(F32)).astype(BF16)
+                inner(h, w, t).start()
+
     def finish(t):
         for h in range(2):
-            for d in (1, 3, 2):
-                second(h, d, t).wait_recv()
+            for w in range(2):
+                inner(h, w, t).wait_recv()
             for i in range(2):
-                for ii in range(2):
-                    total = tbuf[h, t, i, ii]
-                    for d in range(3):
-                        total = total + rbuf[h, d, t, i, ii].astype(F32)
-                    hbuf[t, pl.ds((i * 4 + h * 2 + ii) * 16, 16), :] = total.astype(BF16)
+                total = tbuf[h, t, i] + grecv[h, i, t].astype(F32) + rbuf[h, 1 - i, t, 1].astype(F32)
+                hbuf[t, pl.ds((i * 2 + h) * 32, 32), :] = total.reshape(32, NNU).astype(BF16)
 
     def chunk(t, _):
         mu0 = chunk_row(t) * 2
@@ -222,21 +228,26 @@
         for h in range(2):
             for w in range(2):
                 pair_copy(h * 2 + w, t).wait_recv()
-            for d in (2, 1, 3, 0):
+
+            def total(d, i, h=h):
                 a = lax.rem(place(1 - h) + d, 4)
-                for i in range(2):
-                    for ii in range(2):
-                        total = sums[h, mu0 + i, ii, a] + crecv[h * 2 + a // 2, t, i, ii, lax.rem(a, 2)].astype(F32)
-                        if d == 0:
-                            tbuf[h, t, i, ii] = total
-                        else:
-                            sbuf[h, d - 1, t, i, ii] = total.astype(BF16)
-                if d > 0:
-                    second(h, d, t).start()
+                return sums[h, mu0 + i, :, a] + crecv[h * 2 + a // 2, t, i, :, lax.rem(a, 2)].astype(F32)
+            for w in range(2):
+                sbuf[h, w, t, 0] = total(2, w).astype(BF16)
+                sbuf[h, w, t, 1] = total(1 + 2 * w, 1 - w).astype(BF16)
+                outer(h, w, t).start()
+            for w in range(2):
+                keep[h, w, t] = total(1 + 2 * w, w)
+            for i in range(2):
+                tbuf[h, t, i] = total(0, i)
 
         @pl.when(t < CHUNKS - AHEAD)
         def _():
             start_pair(t + AHEAD)
+
+        @pl.when(t >= 1)
+        def _():
+            forward(t - 1)
 
         @pl.when(t >= LAG)
         def _():
@@ -244,6 +255,7 @@
             third(t - LAG).start()
         return 0
     lax.fori_loop(0, CHUNKS, chunk, 0)
+    forward(CHUNKS - 1)
 
     for t in range(CHUNKS - LAG, 7):
         finish(t)
@@ -261,15 +273,16 @@
     o_ref[row] = jnp.dot(virt, hbuf[7], preferred_element_type=F32).astype(BF16)
     last_body(6, 0)
 
-    for copy in tabs.values():
+    for copy in [*cs.values(), *tabs.values()]:
         copy.wait_send()
 
     def sent_body(t, _):
         for u in range(4):
             pair_copy(u, t).wait_send()
         for h in range(2):
-            for d in range(1, 4):
-                second(h, d, t).wait_send()
+            for w in range(2):
+                outer(h, w, t).wait_send()
+                inner(h, w, t).wait_send()
 
         @pl.when(t < 7)
         def _():
@@ -303,15 +316,19 @@
             pltpu.VMEM((4, CHUNKS, 2, 2, 2, 16, NNU), BF16),
             pltpu.VMEM((4, CHUNKS, 2, 2, 2, 16, NNU), BF16),
             pltpu.VMEM((2, CHUNKS, 2, 2, 16, NNU), F32),
-            pltpu.VMEM((2, 3, CHUNKS, 2, 2, 16, NNU), BF16),
-            pltpu.VMEM((2, 3, CHUNKS, 2, 2, 16, NNU), BF16),
+            pltpu.VMEM((2, 2, CHUNKS, 2, 2, 16, NNU), BF16),
+            pltpu.VMEM((2, 2, CHUNKS, 2, 2, 16, NNU), BF16),
+            pltpu.VMEM((2, 2, CHUNKS, 2, 16, NNU), F32),
+            pltpu.VMEM((2, 2, CHUNKS, 2, 16, NNU), BF16),
+            pltpu.VMEM((2, 2, CHUNKS, 2, 16, NNU), BF16),
             pltpu.VMEM((8, 128, NNU), BF16),
             pltpu.VMEM((8, 128, NNU), BF16),
             pltpu.VMEM((8, 128), jnp.int32),
             pltpu.VMEM((5, 8, 128), jnp.int32),
             pltpu.SMEM((5, 8, 128), jnp.int32),
             dma, dma((2, 3)), dma((2, 2)), dma((2, 2)), dma((2, 2)), dma((2, 2)), dma((2, 2)), dma((2, 2)), dma,
-            dma((4, CHUNKS)), dma((4, CHUNKS)), dma((2, 3, CHUNKS)), dma((2, 3, CHUNKS)), dma((7,)), dma((7,)),
+            dma((4, CHUNKS)), dma((4, CHUNKS)), dma((2, 2, CHUNKS)), dma((2, 2, CHUNKS)),
+            dma((2, 2, CHUNKS)), dma((2, 2, CHUNKS)), dma((7,)), dma((7,)),
         ],
         compiler_params=pltpu.CompilerParams(
             collective_id=0, has_side_effects=True, vmem_limit_bytes=60 << 20),

time: 78.1 us -> 73.1 us (0.936)
  Pallas kernels: 75.5 us -> 70.8 us
    pallas_call x1, Pallas kernels: 75.5 us -> 70.8 us  [local(): pl.pallas_call(kernel, out_shape=jax.ShapeDtypeStruct((8, 128, NNU), BF16...]
where the time goes in v4:
time: 73.1 us; the launch traced here: 72.9 us
  Pallas kernels  70.8 us (97%)
  local copies, waits for them, and re-layouts  2.09 us (3%)
    pallas_call x1, Pallas kernels, local(): pl.pallas_call(kernel, out_shape=jax.ShapeDtypeStruct((8, 128, NNU), BF16...  70.8 us
    unnamed x1, local copies, waits for them, and re-layouts  2.09 us

profile of v4, /device:TPU:1, one launch (start us, length us, event | category | flops | bytes accessed | tf_op | source)
XLA Modules:
  0.0 72.9 jit_solution(14160324973390975044)
XLA Ops:
  0.0 70.8 %density_transform.1 = bf16[8,128,384]{2,1,0:T(8,128)(2,1)} custom-call(bf16[4,4,64,4096]{3,2,1,0:T(8,128)(2,1)} %bitcast.7, s32[1,64]{1,0:T(1,128)} %bitcast.10, s32[1,64]{1,0:T(1,128)} %bitcast.11, bf16[128,64,384]{2,1,0:T(8,128)(2,1)} %bitcast.8, bf16[128,128]{1,0:T(8,128)(2,1)} %virt_ref.1), custom_call_target="tpu_custom_call" | custom-call | tf_op jit(solution)/shard_map/density_transform/pallas_call | solution.py:296
  70.8 2.1 %copy.8 = bf16[8,1,128,384]{3,2,1,0:T(8,128)(2,1)} copy(bf16[8,1,128,384]{3,2,1,0:T(8,128)(2,1)} %bitcast.9) | data formatting | bytes 1572864

commit v5 on v4

--- a/solution.py
+++ b/solution.py
@@ -14,7 +14,7 @@
 PAIRS = 64
 CHUNKS = 8
 EARLY = 3
-AHEAD = 4
+AHEAD = 3
 LAG = 3
 HALF = 2048
 F32 = jnp.float32
@@ -38,9 +38,9 @@
     return jnp.where(row == 0, source, target)
 
 
-def kernel(t_ref, mu_ref, nu_ref, occ_ref, virt_ref, o_ref,
-           own, arr_c, arr_d, occ, xown, xt, sums, csums, cbuf, crecv, tbuf, sbuf, rbuf, keep, gown, grecv, hbuf, gbuf, tab_v, tab_r, tab_s,
-           occ_sem, own_sem, sc, rc, sd, rd, st, rt, tab_sem, sp, rp, s2, r2, sg, rg, s3, r3):
+def kernel(t_ref, mu_hbm, nu_hbm, occ_ref, virt_hbm, out_ref,
+           mu_ref, nu_ref, virt_ref, o_ref, own, arr_c, arr_d, occ, xown, xt, sums, csums, cbuf, crecv, tbuf, sbuf, rbuf, keep, gown, grecv, hbuf, gbuf, tab_v, tab_r, tab_s,
+           occ_sem, own_sem, sc, rc, sd, rd, st, rt, tab_sem, sp, rp, s2, r2, sg, rg, s3, r3, sl, rl, small_sem, out_sem):
     row, col = lax.axis_index("row"), lax.axis_index("col")
     x, y, z, core = col // 4, col % 4, row // 2, row % 2
 
@@ -61,6 +61,18 @@
             return t_ref.at[lax.rem(x + d, 4), pl.ds(first, count), :, pl.ds(0, HALF)]
         return t_ref.at[pl.ds(first, count), lax.rem(y + d, 4), :, pl.ds(HALF, HALF)]
 
+    barrier = pltpu.get_barrier_semaphore()
+    for d in range(1, 4):
+        pl.semaphore_signal(barrier, inc=1, device_id=at_x(d), device_id_type=MESH)
+        pl.semaphore_signal(barrier, inc=1, device_id=at_y(d), device_id_type=MESH)
+    for d in range(1, 8):
+        pl.semaphore_signal(barrier, inc=1, device_id=(lax.rem(row + d, 8), col), device_id_type=MESH)
+
+    small = []
+    for k, (src, dst) in enumerate(((mu_hbm, mu_ref), (nu_hbm, nu_ref), (virt_hbm, virt_ref))):
+        copy = pltpu.make_async_copy(src, dst, small_sem.at[k])
+        copy.start()
+        small.append(copy)
     locals_ = []
     for h in range(2):
         for k, (d, first, count, at) in enumerate(((0, 0, 4, 0), (1, 0, 2, 4), (3, 2, 2, 6))):
@@ -70,12 +82,6 @@
     occ_copy = pltpu.make_async_copy(occ_ref, occ.at[pl.ds(0, NBNU)], occ_sem)
     occ_copy.start()
 
-    barrier = pltpu.get_barrier_semaphore()
-    for d in range(1, 4):
-        pl.semaphore_signal(barrier, inc=1, device_id=at_x(d), device_id_type=MESH)
-        pl.semaphore_signal(barrier, inc=1, device_id=at_y(d), device_id_type=MESH)
-    for d in range(1, 8):
-        pl.semaphore_signal(barrier, inc=1, device_id=(lax.rem(row + d, 8), col), device_id_type=MESH)
     pl.semaphore_wait(barrier, 13)
 
     cs, ds, tabs = {}, {}, {}
@@ -89,6 +95,8 @@
                 device_id=ring(h, 1 + 2 * w), device_id_type=MESH)
             cs[h, w].start()
 
+    for copy in small:
+        copy.wait()
     tab_v[...] = slot_table(mu_ref[...], nu_ref[...])
     tab_r[4] = tab_v[...]
     for w in range(2):
@@ -181,6 +189,8 @@
         copy.wait_send()
     for t in range(EARLY, AHEAD):
         start_pair(t)
+    for copy in [*cs.values(), *tabs.values()]:
+        copy.wait_send()
     for u in range(4):
         ds[u // 2, u % 2].wait_recv()
         relayout(arr_d.at[u], xt.at[u], 2)
@@ -201,6 +211,13 @@
             src_ref=gown.at[h, w, t], dst_ref=grecv.at[h, w, t], send_sem=sg.at[h, w, t], recv_sem=rg.at[h, w, t],
             device_id=ring(1 - h, 1 + 2 * w), device_id_type=MESH)
 
+    LAST = CHUNKS - 1
+
+    def straight(h, w, k):
+        return pltpu.make_async_remote_copy(
+            src_ref=sbuf.at[h, w, LAST, k], dst_ref=rbuf.at[h, w, LAST, k], send_sem=sl.at[h, w, k], recv_sem=rl.at[h, w, k],
+            device_id=ring(1 - h, 2 if k == 0 else 1 + 2 * w), device_id_type=MESH)
+
     def third(t):
         return pltpu.make_async_remote_copy(
             src_ref=hbuf.at[t], dst_ref=gbuf.at[row], send_sem=s3.at[t], recv_sem=r3.at[t],
@@ -209,25 +226,30 @@
     def forward(t):
         for h in range(2):
             for w in range(2):
-                outer(h, w, t).wait_recv()
+                outer(h, w, t).wait()
                 gown[h, w, t] = (keep[h, w, t] + rbuf[h, w, t, 0].astype(F32)).astype(BF16)
                 inner(h, w, t).start()
 
-    def finish(t):
-        for h in range(2):
-            for w in range(2):
-                inner(h, w, t).wait_recv()
+    def finish(t, last=False):
+        for h in range(2):
+            for w in range(2):
+                inner(h, w, t).wait()
+                if last:
+                    for k in range(2):
+                        straight(h, w, k).wait()
             for i in range(2):
                 total = tbuf[h, t, i] + grecv[h, i, t].astype(F32) + rbuf[h, 1 - i, t, 1].astype(F32)
+                if last:
+                    total = total + rbuf[h, i, t, 0].astype(F32)
                 hbuf[t, pl.ds((i * 2 + h) * 32, 32), :] = total.reshape(32, NNU).astype(BF16)
 
-    def chunk(t, _):
+    def chunk(t, last):
         mu0 = chunk_row(t) * 2
         for i in range(2):
             direct(mu0 + i)
         for h in range(2):
             for w in range(2):
-                pair_copy(h * 2 + w, t).wait_recv()
+                pair_copy(h * 2 + w, t).wait()
 
             def total(d, i, h=h):
                 a = lax.rem(place(1 - h) + d, 4)
@@ -235,11 +257,22 @@
             for w in range(2):
                 sbuf[h, w, t, 0] = total(2, w).astype(BF16)
                 sbuf[h, w, t, 1] = total(1 + 2 * w, 1 - w).astype(BF16)
-                outer(h, w, t).start()
-            for w in range(2):
-                keep[h, w, t] = total(1 + 2 * w, w)
+                if last:
+                    for k in range(2):
+                        straight(h, w, k).start()
+                else:
+                    outer(h, w, t).start()
+            for w in range(2):
+                if last:
+                    gown[h, w, t] = total(1 + 2 * w, w).astype(BF16)
+                    inner(h, w, t).start()
+                else:
+                    keep[h, w, t] = total(1 + 2 * w, w)
             for i in range(2):
                 tbuf[h, t, i] = total(0, i)
+
+    def chunk_body(t, _):
+        chunk(t, False)
 
         @pl.when(t < CHUNKS - AHEAD)
         def _():
@@ -254,41 +287,34 @@
             finish(t - LAG)
             third(t - LAG).start()
         return 0
-    lax.fori_loop(0, CHUNKS, chunk, 0)
-    forward(CHUNKS - 1)
-
-    for t in range(CHUNKS - LAG, 7):
+    lax.fori_loop(0, LAST, chunk_body, 0)
+    chunk(LAST, True)
+    forward(LAST - 1)
+    for t in range(LAST - LAG, LAST):
         finish(t)
         third(t).start()
 
+    def out_copy(g):
+        return pltpu.make_async_copy(o_ref.at[g], out_ref.at[g], out_sem.at[g])
+
+    def emit(g, half):
+        o_ref[g] = jnp.dot(virt, half, preferred_element_type=F32).astype(BF16)
+        out_copy(g).start()
+
     def last_body(t, _):
         g = lax.rem(z + 3 - t // 2, 4) * 2 + lax.rem(t + 1 + core, 2)
+        third(t).wait_send()
         pltpu.make_async_remote_copy(
             src_ref=hbuf.at[t], dst_ref=gbuf.at[g], send_sem=s3.at[t], recv_sem=r3.at[t],
             device_id=(row, col), device_id_type=MESH).wait_recv()
-        o_ref[g] = jnp.dot(virt, gbuf[g], preferred_element_type=F32).astype(BF16)
+        emit(g, gbuf[g])
         return 0
     lax.fori_loop(0, 6, last_body, 0)
-    finish(7)
-    o_ref[row] = jnp.dot(virt, hbuf[7], preferred_element_type=F32).astype(BF16)
     last_body(6, 0)
-
-    for copy in [*cs.values(), *tabs.values()]:
-        copy.wait_send()
-
-    def sent_body(t, _):
-        for u in range(4):
-            pair_copy(u, t).wait_send()
-        for h in range(2):
-            for w in range(2):
-                outer(h, w, t).wait_send()
-                inner(h, w, t).wait_send()
-
-        @pl.when(t < 7)
-        def _():
-            third(t).wait_send()
-        return 0
-    lax.fori_loop(0, CHUNKS, sent_body, 0)
+    finish(LAST, True)
+    emit(row, hbuf[LAST])
+    for g in range(8):
+        out_copy(g).wait()
 
 
 def local(tensor, pair_mu, pair_nu, occ_density, virt_density):
@@ -298,13 +324,13 @@
         out_shape=jax.ShapeDtypeStruct((8, 128, NNU), BF16),
         in_specs=[
             pl.BlockSpec(memory_space=pl.ANY),
-            pl.BlockSpec(memory_space=pltpu.VMEM),
-            pl.BlockSpec(memory_space=pltpu.VMEM),
-            pl.BlockSpec(memory_space=pl.ANY),
-            pl.BlockSpec(memory_space=pltpu.VMEM),
-        ],
-        out_specs=pl.BlockSpec(memory_space=pltpu.VMEM),
+        ] * 5,
+        out_specs=pl.BlockSpec(memory_space=pl.ANY),
         scratch_shapes=[
+            pltpu.VMEM((1, PAIRS), jnp.int32),
+            pltpu.VMEM((1, PAIRS), jnp.int32),
+            pltpu.VMEM((128, 128), BF16),
+            pltpu.VMEM((8, 128, NNU), BF16),
             pltpu.VMEM((2, 8, PAIRS, HALF), BF16),
             pltpu.VMEM((4, 2, PAIRS, HALF), BF16),
             pltpu.VMEM((4, 2, PAIRS, HALF), BF16),
@@ -328,7 +354,8 @@
             pltpu.SMEM((5, 8, 128), jnp.int32),
             dma, dma((2, 3)), dma((2, 2)), dma((2, 2)), dma((2, 2)), dma((2, 2)), dma((2, 2)), dma((2, 2)), dma,
             dma((4, CHUNKS)), dma((4, CHUNKS)), dma((2, 2, CHUNKS)), dma((2, 2, CHUNKS)),
-            dma((2, 2, CHUNKS)), dma((2, 2, CHUNKS)), dma((7,)), dma((7,)),
+            dma((2, 2, CHUNKS)), dma((2, 2, CHUNKS)), dma((7,)), dma((7,)), dma((2, 2, 2)), dma((2, 2, 2)),
+            dma((3,)), dma((8,)),
         ],
         compiler_params=pltpu.CompilerParams(
             collective_id=0, has_side_effects=True, vmem_limit_bytes=60 << 20),

time: 73.1 us -> 71.4 us (0.977)
  Pallas kernels: 70.8 us -> 69.1 us
    pallas_call x1, Pallas kernels: 70.8 us -> 69.1 us  [local(): pl.pallas_call(kernel, out_shape=jax.ShapeDtypeStruct((8, 128, NNU), BF16...]
where the time goes in v5:
time: 71.4 us; the launch traced here: 71.2 us
  Pallas kernels  69.1 us (97%)
  local copies, waits for them, and re-layouts  2.09 us (3%)
    pallas_call x1, Pallas kernels, local(): pl.pallas_call(kernel, out_shape=jax.ShapeDtypeStruct((8, 128, NNU), BF16...  69.1 us
    unnamed x1, local copies, waits for them, and re-layouts  2.09 us

profile of v5, /device:TPU:1, one launch (start us, length us, event | category | flops | bytes accessed | tf_op | source)
XLA Modules:
  0.0 71.2 jit_solution(4250821592797838972)
XLA Ops:
  0.0 69.1 %density_transform.1 = bf16[8,128,384]{2,1,0:T(8,128)(2,1)} custom-call(bf16[4,4,64,4096]{3,2,1,0:T(8,128)(2,1)} %bitcast.7, s32[1,64]{1,0:T(1,128)} %bitcast.10, s32[1,64]{1,0:T(1,128)} %bitcast.11, bf16[128,64,384]{2,1,0:T(8,128)(2,1)} %bitcast.8, bf16[128,128]{1,0:T(8,128)(2,1)} %virt_hbm.1), custom_call_target="tpu_custom_call" | custom-call | tf_op jit(solution)/shard_map/density_transform/pallas_call | solution.py:322
  69.1 2.1 %copy.8 = bf16[8,1,128,384]{3,2,1,0:T(8,128)(2,1)} copy(bf16[8,1,128,384]{3,2,1,0:T(8,128)(2,1)} %bitcast.9) | data formatting | bytes 1572864

commit v6 on v5

--- a/solution.py
+++ b/solution.py
@@ -38,8 +38,8 @@
     return jnp.where(row == 0, source, target)
 
 
-def kernel(t_ref, mu_hbm, nu_hbm, occ_ref, virt_hbm, out_ref,
-           mu_ref, nu_ref, virt_ref, o_ref, own, arr_c, arr_d, occ, xown, xt, sums, csums, cbuf, crecv, tbuf, sbuf, rbuf, keep, gown, grecv, hbuf, gbuf, tab_v, tab_r, tab_s,
+def kernel(t_ref, mu_hbm, nu_hbm, occ_ref, out_ref,
+           mu_ref, nu_ref, own, arr_c, arr_d, occ, xown, xt, sums, csums, cbuf, crecv, tbuf, sbuf, rbuf, keep, gown, grecv, hbuf, gbuf, tab_v, tab_r, tab_s,
            occ_sem, own_sem, sc, rc, sd, rd, st, rt, tab_sem, sp, rp, s2, r2, sg, rg, s3, r3, sl, rl, small_sem, out_sem):
     row, col = lax.axis_index("row"), lax.axis_index("col")
     x, y, z, core = col // 4, col % 4, row // 2, row % 2
@@ -69,7 +69,7 @@
         pl.semaphore_signal(barrier, inc=1, device_id=(lax.rem(row + d, 8), col), device_id_type=MESH)
 
     small = []
-    for k, (src, dst) in enumerate(((mu_hbm, mu_ref), (nu_hbm, nu_ref), (virt_hbm, virt_ref))):
+    for k, (src, dst) in enumerate(((mu_hbm, mu_ref), (nu_hbm, nu_ref))):
         copy = pltpu.make_async_copy(src, dst, small_sem.at[k])
         copy.start()
         small.append(copy)
@@ -107,11 +107,6 @@
             copy.start()
             tabs[h, w] = copy
     occ[NBNU] = jnp.zeros((BS, NNU), BF16)
-    c = lax.broadcasted_iota(jnp.int32, (128, 128), 1)
-    r = lax.broadcasted_iota(jnp.int32, (128, 128), 0)
-    from_col = (c // 64) * 64 + ((c // 32) % 2) * 32 + (c % 16) * 2 + (c // 16) % 2
-    perm = jnp.where(r == from_col, 1.0, 0.0).astype(BF16)
-    virt = jnp.dot(virt_ref[...], perm, preferred_element_type=F32).astype(BF16)
 
     def relayout(src, dst, aux_count):
         def body(i, _):
@@ -294,12 +289,8 @@
         finish(t)
         third(t).start()
 
-    def out_copy(g):
-        return pltpu.make_async_copy(o_ref.at[g], out_ref.at[g], out_sem.at[g])
-
-    def emit(g, half):
-        o_ref[g] = jnp.dot(virt, half, preferred_element_type=F32).astype(BF16)
-        out_copy(g).start()
+    def out_copy(src, g):
+        return pltpu.make_async_copy(src, out_ref.at[g], out_sem.at[g])
 
     def last_body(t, _):
         g = lax.rem(z + 3 - t // 2, 4) * 2 + lax.rem(t + 1 + core, 2)
@@ -307,30 +298,38 @@
         pltpu.make_async_remote_copy(
             src_ref=hbuf.at[t], dst_ref=gbuf.at[g], send_sem=s3.at[t], recv_sem=r3.at[t],
             device_id=(row, col), device_id_type=MESH).wait_recv()
-        emit(g, gbuf[g])
+        out_copy(gbuf.at[g], g).start()
         return 0
     lax.fori_loop(0, 6, last_body, 0)
     last_body(6, 0)
     finish(LAST, True)
-    emit(row, hbuf[LAST])
+    out_copy(hbuf.at[LAST], row).start()
     for g in range(8):
-        out_copy(g).wait()
+        out_copy(gbuf.at[g], g).wait()
+
+
+def virt_kernel(virt_ref, half_ref, o_ref):
+    c = lax.broadcasted_iota(jnp.int32, (128, 128), 1)
+    r = lax.broadcasted_iota(jnp.int32, (128, 128), 0)
+    from_col = (c // 64) * 64 + ((c // 32) % 2) * 32 + (c % 16) * 2 + (c // 16) % 2
+    perm = jnp.where(r == from_col, 1.0, 0.0).astype(BF16)
+    virt = jnp.dot(virt_ref[...], perm, preferred_element_type=F32).astype(BF16)
+    for g in range(4):
+        o_ref[g] = jnp.dot(virt, half_ref[g], preferred_element_type=F32).astype(BF16)
 
 
 def local(tensor, pair_mu, pair_nu, occ_density, virt_density):
     dma = pltpu.SemaphoreType.DMA
-    out = pl.pallas_call(
+    halves = pl.pallas_call(
         kernel,
         out_shape=jax.ShapeDtypeStruct((8, 128, NNU), BF16),
         in_specs=[
             pl.BlockSpec(memory_space=pl.ANY),
-        ] * 5,
+        ] * 4,
         out_specs=pl.BlockSpec(memory_space=pl.ANY),
         scratch_shapes=[
             pltpu.VMEM((1, PAIRS), jnp.int32),
             pltpu.VMEM((1, PAIRS), jnp.int32),
-            pltpu.VMEM((128, 128), BF16),
-            pltpu.VMEM((8, 128, NNU), BF16),
             pltpu.VMEM((2, 8, PAIRS, HALF), BF16),
             pltpu.VMEM((4, 2, PAIRS, HALF), BF16),
             pltpu.VMEM((4, 2, PAIRS, HALF), BF16),
@@ -355,7 +354,7 @@
             dma, dma((2, 3)), dma((2, 2)), dma((2, 2)), dma((2, 2)), dma((2, 2)), dma((2, 2)), dma((2, 2)), dma,
             dma((4, CHUNKS)), dma((4, CHUNKS)), dma((2, 2, CHUNKS)), dma((2, 2, CHUNKS)),
             dma((2, 2, CHUNKS)), dma((2, 2, CHUNKS)), dma((7,)), dma((7,)), dma((2, 2, 2)), dma((2, 2, 2)),
-            dma((3,)), dma((8,)),
+            dma((2,)), dma((8,)),
         ],
         compiler_params=pltpu.CompilerParams(
             collective_id=0, has_side_effects=True, vmem_limit_bytes=60 << 20),
@@ -365,8 +364,15 @@
         pair_mu.reshape(1, PAIRS),
         pair_nu.reshape(1, PAIRS),
         occ_density.reshape(NBNU, BS, NNU),
-        virt_density,
     )
+    out = pl.pallas_call(
+        virt_kernel,
+        out_shape=jax.ShapeDtypeStruct((8, 128, NNU), BF16),
+        grid=(2,),
+        in_specs=[pl.BlockSpec((128, 128), lambda g: (0, 0)), pl.BlockSpec((4, 128, NNU), lambda g: (g, 0, 0))],
+        out_specs=pl.BlockSpec((4, 128, NNU), lambda g: (g, 0, 0)),
+        name="virt_product",
+    )(virt_density, halves)
     return out.reshape(8, 1, 128, NNU)
 
 

time: 71.4 us -> 71.5 us (level)
  Pallas kernels: 69.1 us -> 71.3 us
  local copies, waits for them, and re-layouts: 2.09 us -> 0 us
    pallas_call x0 -> x1, Pallas kernels: none -> 2.55 us  [local(): pl.pallas_call(virt_kernel, out_shape=jax.ShapeDtypeStruct((8, 128, NNU),...]
    unnamed x1 -> x0, local copies, waits for them, and re-layouts: 2.09 us -> none
where the time goes in v6:
time: 71.5 us; the launch traced here: 71.3 us
  Pallas kernels  71.3 us (100%)
    pallas_call x1, Pallas kernels, local(): pl.pallas_call(kernel, out_shape=jax.ShapeDtypeStruct((8, 128, NNU), BF16...  68.8 us
    pallas_call x1, Pallas kernels, local(): pl.pallas_call(virt_kernel, out_shape=jax.ShapeDtypeStruct((8, 128, NNU),...  2.55 us

profile of v6, /device:TPU:1, one launch (start us, length us, event | category | flops | bytes accessed | tf_op | source)
XLA Modules:
  0.0 71.3 jit_solution(7390431746064616514)
XLA Ops:
  0.0 68.8 %density_transform.1.half_ref = bf16[8,128,384]{2,1,0:T(8,128)(2,1)} custom-call(bf16[4,4,64,4096]{3,2,1,0:T(8,128)(2,1)} %bitcast.7, s32[1,64]{1,0:T(1,128)} %bitcast.9, s32[1,64]{1,0:T(1,128)} %bitcast.10, bf16[128,64,384]{2,1,0:T(8,128)(2,1)} %bitcast.8), custom_call_target="tpu_custom_call" | custom-call | tf_op jit(solution)/shard_map/density_transform/pallas_call | solution.py:323
  68.8 2.6 %virt_product.1 = bf16[8,128,384]{2,1,0:T(8,128)(2,1)} custom-call(bf16[128,128]{1,0:T(8,128)(2,1)} %virt_ref.1, bf16[8,128,384]{2,1,0:T(8,128)(2,1)} %density_transform.1.half_ref), custom_call_target="tpu_custom_call" | custom-call | tf_op jit(solution)/shard_map/virt_product/pallas_call | solution.py:368
